TPU v7x, 32 devices: a whole 2x2x4 slice. The times are simulated.
32 devices in a mesh: groups: 2 (over y), dp: 4 (over z), mp: 4 (over x, core).
Axes of the slice: x: 2, y: 2, z: 4, core: 2. Of those that a mesh axis runs over, the one named last changes fastest.
Arguments:
- activations: bfloat16 [16, 128, 28672], P(('groups', 'dp'), None, 'mp'), parts along dimension 0
- output_gradients: bfloat16 [16, 128, 8192], P(('groups', 'dp'), None, 'mp'), parts along dimension 0
- counts: int32 [16], P(('groups', 'dp')), parts along dimension 0, may hold values from 32 to 128, as said below
- left_factors: bfloat16 [256, 8192], P('dp', 'mp'), may hold values from -0.0625 to 0.0625
- right_factors: bfloat16 [256, 28672], P('dp', 'mp'), may hold values from -0.03125 to 0.03125
Outputs:
- scores: float32 [16, 8], P(('groups', 'dp')), parts along dimension 0
- grad_rms: float32 [16], P(('groups', 'dp')), parts along dimension 0
There are 2 independent parts, one for each index of `groups`. A program takes and returns all parts, laid end to end along the dimension named above; an argument that names none is the same for every part. Nothing has to cross between parts.
Inputs may be any that keep to these rules, and one draw needn't show every extreme that they name: `counts`: some training sequence has all 128 slots filled and some has 32.
All inputs are finite; a program needn't handle non-finite values.
Results may differ from a plain program's by a relative error of at most 0.0003.
Values may be sent and summed in bfloat16 or wider, within the bound.
A program may use at most 64 MiB of HBM per device.

v0:
```python
import jax
import jax.numpy as jnp
from jax import lax
from jax.sharding import PartitionSpec as P

D = 8192
FF = 28672
RANK = 32


epsilon = 1e-06


def contract_last(left_side, right_side):
    return lax.dot_general(
        left_side, right_side, (((1,), (1,)), ((), ())), preferred_element_type=jnp.float32
    )


def shards(activations, output_gradients, counts, left_factors, right_factors):
    seq_dev, length, ff_local = activations.shape
    local_model_width = output_gradients.shape[2]
    row_count = seq_dev * length
    act_rows = activations.reshape(row_count, ff_local)
    grad_rows = output_gradients.reshape(row_count, local_model_width)
    qcols_all = left_factors.shape[0] * lax.axis_size("dp")
    positions = lax.broadcasted_iota(jnp.int32, (seq_dev, length), 1)
    token_mask = (positions < counts[:, None]).astype(jnp.float32)
    pair_mask = token_mask[:, :, None] * token_mask[:, None, :]
    token_mask = token_mask.reshape(row_count)
    left_all, right_all = (
        lax.all_gather(left_factors, "dp", axis=0, tiled=True),
        lax.all_gather(right_factors, "dp", axis=0, tiled=True),
    )
    grad_proj = contract_last(grad_rows, left_all)
    act_proj = contract_last(act_rows, right_all)
    gradient_covariance = jnp.einsum(
        "anr,ayr->any", output_gradients, output_gradients, preferred_element_type=jnp.float32
    )
    act_gram = jnp.einsum(
        "slf,smf->slm", activations, activations, preferred_element_type=jnp.float32
    )
    grad_proj, gradient_covariance = lax.psum((grad_proj, gradient_covariance), "mp")
    token_terms = grad_proj * act_proj * token_mask[:, None]
    score_part = token_terms.reshape(seq_dev, length, qcols_all // RANK, RANK).sum(axis=(1, 3))
    norm_portion = jnp.sum(gradient_covariance * act_gram * pair_mask, axis=(1, 2))
    raw_score, norm_sq = lax.psum((score_part, norm_portion), "mp")
    grad_rms = jnp.sqrt(norm_sq / (D * FF) + epsilon)
    return (raw_score / grad_rms[:, None], grad_rms)


def solution(mesh):
    placed = (
        P(("groups", "dp"), None, "mp"),
        P(("groups", "dp"), None, "mp"),
        P(("groups", "dp")),
        P("dp", "mp"),
        P("dp", "mp"),
    )
    return jax.shard_map(
        shards,
        mesh=mesh,
        in_specs=placed,
        out_specs=(P(("groups", "dp"), None), P(("groups", "dp"))),
        check_vma=False,
    )
```

profile of v0, /device:TPU:0, one launch (start us, length us, event | category | flops | bytes accessed | tf_op | source)
XLA Modules:
  0.0 167.8 jit_solution(1293497749247898828)
XLA Ops:
  7.2 0.0 copy-start
  7.2 0.0 copy-start.1
  7.2 0.0 all-gather.3.cloned.1.call-start
  7.2 0.7 all-gather.3.cloned.1.call-update
  7.9 0.0 all-reduce.4.cloned.1.call-start
  8.0 0.4 copy-done
  8.4 1.1 fusion.5
  9.5 30.8 %all-gather.3.cloned.1.call-done = bf16[256,2048]{1,0:T(8,128)(2,1)} async-done(((bf16[64,2048]{1,0:T(8,128)(2,1)}), bf16[256,2048]{1,0:T(8,128)(2,1)}) %all-gather.3.cloned.1.call-update) | async-done | bytes 1048592 | tf_op jit(solution)/shard_map/all_gather | solution.py:32
  40.3 2.4 %fusion.4 = f32[256,256]{1,0:T(8,128)} fusion(bf16[256,2048]{1,0:T(8,128)(2,1)S(1)} %bitcast.14, bf16[256,2048]{1,0:T(8,128)(2,1)} %all-gather.3.cloned.1.call-done), kind=kOutput, calls=%fused_computation.9 | convolution fusion | flops 268435456 | bytes 2359296 | tf_op jit(solution)/shard_map/dot_general | solution.py:15
  42.6 0.0 all-reduce.4.cloned.1.call-update
  42.7 0.0 all-gather.5.cloned.1.call-start
  42.7 0.7 all-gather.5.cloned.1.call-update
  43.4 0.0 copy-done.1
  43.4 0.1 compare_convert_fusion
  43.5 31.5 %all-reduce.4.cloned.1.call-done = (f32[256,256]{1,0:T(8,128)}, f32[2,128,128]{2,1,0:T(8,128)}) async-done(((f32[256,256]{1,0:T(8,128)}, f32[2,128,128]{2,1,0:T(8,128)}), (f32[256,256]{1,0:T(8,128)}, f32[2,128,128]{2,1,0:T(8,128)})) %all-reduce.4.cloned.1.call-update) | async-done | bytes 393232 | tf_op jit(solution)/shard_map/psum | solution.py:43
  74.9 0.0 copy-start.3
  74.9 4.4 %fusion.2 = f32[2]{0:T(128)S(1)} fusion(f32[2,128,128]{2,1,0:T(8,128)} %get-tuple-element.7, bf16[2,128,7168]{2,1,0:T(8,128)(2,1)} %param.5, f32[2,128]{1,0:T(2,128)S(1)} %get-tuple-element.8), kind=kOutput, calls=%fused_computation.4 | convolution fusion | flops 469893120 | bytes 3802120 | tf_op jit(solution)/shard_map/slf,smf->slm/dot_general | solution.py:40
  79.3 69.4 %all-gather.5.cloned.1.call-done = bf16[256,7168]{1,0:T(8,128)(2,1)} async-done(((bf16[64,7168]{1,0:T(8,128)(2,1)}), bf16[256,7168]{1,0:T(8,128)(2,1)}) %all-gather.5.cloned.1.call-update) | async-done | bytes 3670032 | tf_op jit(solution)/shard_map/all_gather | solution.py:33
  148.8 0.0 copy-done.3
  148.8 4.3 %fusion = f32[256,256]{1,0:T(8,128)S(1)} fusion(f32[256,256]{1,0:T(8,128)S(1)} %copy-done.3, bf16[256,7168]{1,0:T(8,128)(2,1)} %bitcast.15, bf16[256,7168]{1,0:T(8,128)(2,1)} %all-gather.5.cloned.1.call-done, f32[256]{0:T(256)S(1)} %get-tuple-element.9), kind=kOutput, calls=%fused_computation.1 | convolution fusion | flops 939655168 | bytes 7865344 | tf_op jit(solution)/shard_map/dot_general | solution.py:15
  153.1 0.1 copy.8
  153.2 0.1 reshape.66
  153.4 0.2 reduce_sum.18
  153.6 7.0 %all-reduce = (f32[2,8]{0,1:T(8,128)S(1)}, f32[2]{0:T(128)S(1)}) all-reduce(f32[2,8]{0,1:T(8,128)S(1)} %reduce_sum.18, f32[2]{0:T(128)S(1)} %fusion.2), channel_id=1, replica_groups=mesh['groups'=2,'dp'=4,'mp'=4] {'mp'}, use_global_device_ids=true, to_apply=%region_2.0 | all-reduce | flops 18 | bytes 144 | tf_op jit(solution)/shard_map/psum | solution.py:47
  160.6 0.0 copy-start.2
  160.6 0.6 copy.9
  161.3 0.0 copy-done.2
  (2 shorter events, 0.0 us)
Async XLA Ops:
  7.2 1.2 copy-start
  7.2 36.2 %copy-start.1 = (s32[2]{0:T(128)S(1)}, s32[2]{0:T(128)}, u32[]{:S(2)}) copy-start(s32[2]{0:T(128)} %param.7) | copy-start | bytes 28
  7.2 33.1 %all-gather.3.cloned.1.call-start = ((), (), s32[]{:S(2)}) async-start(), calls=%async_computation | async-start | bytes 1310720 | tf_op jit(solution)/shard_map/all_gather | solution.py:32
  7.9 67.0 %all-reduce.4.cloned.1.call-start = ((), (), s32[]{:S(2)}) async-start(), calls=%async_computation.2 | async-start | bytes 786432 | tf_op jit(solution)/shard_map/psum | solution.py:43
  42.7 106.1 %all-gather.5.cloned.1.call-start = ((), (), s32[]{:S(2)}) async-start(), calls=%async_computation.1 | async-start | bytes 4587520 | tf_op jit(solution)/shard_map/all_gather | solution.py:33
  74.9 73.8 %copy-start.3 = (f32[256,256]{1,0:T(8,128)S(1)}, f32[256,256]{1,0:T(8,128)}, u32[]{:S(2)}) copy-start(f32[256,256]{1,0:T(8,128)} %get-tuple-element.6) | copy-start | bytes 786436
  160.6 0.7 copy-start.2
Sparse Core Ops, SparseCore 0:
  9.6 30.6 all-gather.2
  42.8 32.1 all-reduce.3
  76.6 72.1 all-gather.4
where the time goes:
time: 168 us
  waiting for transfers between devices  133 us (79%)
  between operations  13.8 us (8%)
  matrix products  12.2 us (7%)
  blocking collectives  7.02 us (4%)
    all_gather x1, waiting for transfers between devices, shards(): lax.all_gather(right_factors, 'dp', axis=0, tiled=True)  69.4 us
    psum x1, waiting for transfers between devices, shards(): lax.psum((grad_proj, gradient_covariance), 'mp')  31.5 us
    all_gather x1, waiting for transfers between devices, shards(): lax.all_gather(left_factors, 'dp', axis=0, tiled=True)  30.8 us
    psum x1, blocking collectives, shards(): raw_score, norm_sq = lax.psum((score_part, norm_portion), 'mp')  7.02 us
    dot_general x2, matrix products, contract_last(): lax.dot_general(left_side, right_side, (((1,), (1,)), ((), ())), preferre...  6.69 us
    dot_general x1, matrix products, shards(): jnp.einsum('slf,smf->slm', activations, activations, preferred_element_ty...  4.4 us
  transfers between devices with their start and end apart: 3, of which 3 were waited for; matrix products, arithmetic and copies ran while one was open for 3% of the time, Pallas kernels for 0%

commit v1 on v0

--- a/solution.py
+++ b/solution.py
@@ -1,14 +1,20 @@
+import functools
+
 import jax
 import jax.numpy as jnp
 from jax import lax
+from jax.experimental import pallas as pl
+from jax.experimental.pallas import tpu as pltpu
 from jax.sharding import PartitionSpec as P
 
 D = 8192
 FF = 28672
 RANK = 32
-
+AHEAD = 3
+SWAP = 2
 
 epsilon = 1e-06
+MESH = pl.DeviceIdType.MESH
 
 
 def contract_last(left_side, right_side):
@@ -17,7 +23,7 @@
     )
 
 
-def shards(activations, output_gradients, counts, left_factors, right_factors):
+def plain_shards(activations, output_gradients, counts, left_factors, right_factors):
     seq_dev, length, ff_local = activations.shape
     local_model_width = output_gradients.shape[2]
     row_count = seq_dev * length
@@ -49,6 +55,342 @@
     return (raw_score / grad_rms[:, None], grad_rms)
 
 
+def line_kernel(
+    n_left, n_right, width,
+    counts_ref, act_ref, grad_ref, left_ref, right_ref,
+    scores_ref, rms_ref,
+    factors, rows, proj, gram, proj_in, gram_in, tile, tile_in,
+    own_sem, row_sem, out_send, in_send, line_recv, swap_send, swap_recv,
+    proj_send, proj_recv, gram_send, gram_recv, tile_send, tile_recv,
+):
+    pieces = n_left + n_right
+    g, z, m = lax.axis_index("groups"), lax.axis_index("dp"), lax.axis_index("mp")
+    other = 1 - g
+    step_in = 1 - 2 * (z // 2)
+    inner = ((z + 1) // 2) % 2
+    is_inner = inner == 1
+    inward, outward = z + step_in, z - step_in
+    peers = [lax.rem(m + i, 4) for i in (1, 2, 3)]
+
+    def offset(half, piece):
+        if piece < n_left:
+            return (half * n_left + piece) * width
+        return (half * n_right + piece - n_left) * width
+
+    def factor_copy(half, piece):
+        source, at = left_ref if piece < n_left else right_ref, offset(half, piece)
+        return pltpu.make_async_copy(
+            source.at[:, at:at + width], factors.at[z, half, piece], own_sem.at[half, piece]
+        )
+
+    def row_copy(half, piece):
+        source, at = grad_ref if piece < n_left else act_ref, offset(half, piece)
+        return pltpu.make_async_copy(
+            source.at[:, at:at + width], rows.at[half, piece], row_sem.at[half, piece]
+        )
+
+    everything = [(half, piece) for piece in range(pieces) for half in range(2)]
+    for half, piece in everything:
+        factor_copy(half, piece).start()
+    for half, piece in everything:
+        row_copy(half, piece).start()
+
+    barrier = pltpu.get_barrier_semaphore()
+    for i in range(3):
+        pl.semaphore_signal(barrier, inc=1, device_id=(g, z, peers[i]), device_id_type=MESH)
+    pl.semaphore_signal(barrier, inc=1, device_id=(other, z, m), device_id_type=MESH)
+    pl.semaphore_signal(barrier, inc=1, device_id=(g, inward, m), device_id_type=MESH)
+
+    @pl.when(is_inner)
+    def _():
+        pl.semaphore_signal(barrier, inc=1, device_id=(g, outward, m), device_id_type=MESH)
+
+    proj[...] = jnp.zeros_like(proj)
+    gram[...] = jnp.zeros_like(gram)
+    pl.semaphore_wait(barrier, 5 + inner)
+    for half, piece in everything:
+        factor_copy(half, piece).wait()
+
+    def outward_copy(k):
+        block = factors.at[(z + (k // pieces) * step_in) % 4, g, k % pieces]
+        return pltpu.make_async_remote_copy(
+            src_ref=block, dst_ref=block, send_sem=out_send.at[k], recv_sem=line_recv.at[0, k],
+            device_id=(g, (outward + 4) % 4, m), device_id_type=MESH,
+        )
+
+    def inward_copy(k):
+        late = k // pieces
+        source = (z - late * inner * step_in + 4) % 4
+        half = g + (1 - inner) * late * (1 - 2 * g)
+        block = factors.at[source, half, k % pieces]
+        return pltpu.make_async_remote_copy(
+            src_ref=block, dst_ref=block, send_sem=in_send.at[k],
+            recv_sem=line_recv.at[1 - inner, k],
+            device_id=(g, inward, m), device_id_type=MESH,
+        )
+
+    def main_source(k):
+        return (z + (k // pieces + 1) * step_in + 4) % 4
+
+    def arrival(k):
+        block = factors.at[main_source(k), g, k % pieces]
+        return pltpu.make_async_remote_copy(
+            src_ref=block, dst_ref=block, send_sem=out_send.at[k], recv_sem=line_recv.at[0, k],
+            device_id=(g, inward, m), device_id_type=MESH,
+        )
+
+    def minor_arrival(k):
+        late = k // pieces
+        block = factors.at[(outward + 4) % 4, g + late * (1 - 2 * g), k % pieces]
+        return pltpu.make_async_remote_copy(
+            src_ref=block, dst_ref=block, send_sem=out_send.at[k], recv_sem=line_recv.at[1, k],
+            device_id=(g, inward, m), device_id_type=MESH,
+        )
+
+    def swap_copy(k):
+        block = factors.at[main_source(k), g, k % pieces]
+        return pltpu.make_async_remote_copy(
+            src_ref=block, dst_ref=block, send_sem=swap_send.at[k], recv_sem=swap_recv.at[k],
+            device_id=(other, z, m), device_id_type=MESH,
+        )
+
+    def swap_arrival(k):
+        block = factors.at[main_source(k), other, k % pieces]
+        return pltpu.make_async_remote_copy(
+            src_ref=block, dst_ref=block, send_sem=swap_send.at[k], recv_sem=swap_recv.at[k],
+            device_id=(other, z, m), device_id_type=MESH,
+        )
+
+    def proj_copy(i, source):
+        return pltpu.make_async_remote_copy(
+            src_ref=proj.at[0, source], dst_ref=proj_in.at[i, source],
+            send_sem=proj_send.at[i, source], recv_sem=proj_recv.at[i, source],
+            device_id=(g, z, peers[i]), device_id_type=MESH,
+        )
+
+    def gram_copy(i):
+        return pltpu.make_async_remote_copy(
+            src_ref=gram.at[0], dst_ref=gram_in.at[i],
+            send_sem=gram_send.at[i], recv_sem=gram_recv.at[i],
+            device_id=(g, z, peers[i]), device_id_type=MESH,
+        )
+
+    def tile_copy(i):
+        return pltpu.make_async_remote_copy(
+            src_ref=tile, dst_ref=tile_in.at[i],
+            send_sem=tile_send.at[i], recv_sem=tile_recv.at[i],
+            device_id=(g, z, peers[i]), device_id_type=MESH,
+        )
+
+    def project(source, piece):
+        part = contract_last(factors[source, 0, piece], rows[0, piece])
+        part += contract_last(factors[source, 1, piece], rows[1, piece])
+        side = (piece + pieces - n_left) // pieces
+        proj[side, source] += part
+
+    length = rows.shape[2] // 2
+    total = 3 * pieces
+
+    def step(k, carry):
+        @pl.when(k < total)
+        def _():
+            @pl.when(is_inner)
+            def _():
+                @pl.when(k >= AHEAD)
+                def _():
+                    outward_copy(k - AHEAD).wait_send()
+                outward_copy(k).start()
+
+            @pl.when((k >= AHEAD) & (k < 2 * pieces + AHEAD))
+            def _():
+                inward_copy(k - AHEAD).wait_send()
+
+            @pl.when(k < 2 * pieces)
+            def _():
+                inward_copy(k).start()
+
+        @pl.when((k >= AHEAD) & (k < total + AHEAD))
+        def _():
+            j = k - AHEAD
+
+            @pl.when(j < 2 * pieces + (1 - inner) * pieces)
+            def _():
+                arrival(j).wait_recv()
+                swap_copy(j).start()
+
+            @pl.when(j < 2 * pieces * inner)
+            def _():
+                minor_arrival(j).wait_recv()
+
+        @pl.when(k < pieces)
+        def _():
+            for half in range(2):
+                pltpu.make_async_copy(
+                    grad_ref.at[:, 0:width], rows.at[half, k], row_sem.at[half, k]
+                ).wait()
+            project(z, k)
+            side = (k + pieces - n_left) // pieces
+            for seq in range(2):
+                span = slice(seq * length, (seq + 1) * length)
+                first, second = rows[0, k, span, :], rows[1, k, span, :]
+                gram[side, span, :] += contract_last(first, first) + contract_last(second, second)
+
+        @pl.when(k == n_left - 1)
+        def _():
+            for i in range(3):
+                proj_copy(i, z).start()
+                gram_copy(i).start()
+
+        @pl.when(k >= AHEAD + SWAP)
+        def _():
+            j = k - AHEAD - SWAP
+
+            @pl.when(j < 2 * pieces + (1 - inner) * pieces)
+            def _():
+                swap_copy(j).wait_send()
+                swap_arrival(j).wait_recv()
+            project(main_source(j), j % pieces)
+
+            @pl.when(j % pieces == n_left - 1)
+            def _():
+                for i in range(3):
+                    proj_copy(i, main_source(j)).start()
+        return carry
+
+    lax.fori_loop(0, total + AHEAD + SWAP, step, 0)
+
+    token = lax.broadcasted_iota(jnp.int32, (1, length), 1)
+    masks = [(token < counts_ref[seq]).astype(jnp.float32) for seq in range(2)]
+    row_token = lax.broadcasted_iota(jnp.int32, (length, 1), 0)
+    row_masks = [(row_token < counts_ref[seq]).astype(jnp.float32) for seq in range(2)]
+    for i in range(3):
+        gram_copy(i).wait_recv()
+    norms = []
+    for seq in range(2):
+        span = slice(seq * length, (seq + 1) * length)
+        whole = gram[0, span, :] + gram_in[0, span, :] + gram_in[1, span, :] + gram_in[2, span, :]
+        terms = whole * gram[1, span, :] * masks[seq]
+        down = jnp.sum(terms * row_masks[seq], axis=0, keepdims=True)
+        norms.append(jnp.sum(down, axis=1, keepdims=True))
+    for i in range(3):
+        for source in range(4):
+            proj_copy(i, source).wait_recv()
+    columns = proj.shape[2]
+    queries = 4 * columns // RANK
+    mask_row = jnp.concatenate(masks, axis=1)
+    lane = lax.broadcasted_iota(jnp.int32, (1, 128), 1)
+    found = [jnp.zeros((1, 128), jnp.float32) for _ in range(2)]
+    for source in range(4):
+        whole = proj[0, source] + proj_in[0, source] + proj_in[1, source] + proj_in[2, source]
+        terms = whole * proj[1, source] * mask_row
+        for q in range(columns // RANK):
+            down = jnp.sum(terms[q * RANK:(q + 1) * RANK, :], axis=0, keepdims=True)
+            for seq in range(2):
+                value = jnp.sum(down[:, seq * length:(seq + 1) * length], axis=1, keepdims=True)
+                found[seq] += jnp.where(lane == source * (columns // RANK) + q, value, 0.0)
+    tile[...] = jnp.concatenate(
+        found + [jnp.broadcast_to(norms[seq], (1, 128)) for seq in range(2)]
+        + [jnp.zeros((4, 128), jnp.float32)], axis=0
+    )
+    for i in range(3):
+        tile_copy(i).start()
+    for i in range(3):
+        tile_copy(i).wait_recv()
+    whole = tile[...] + tile_in[0] + tile_in[1] + tile_in[2]
+    rms = jnp.sqrt(whole[2:4, :] / (D * FF) + epsilon)
+    scores_ref[...] = (whole[0:2, :] / rms)[:, 0:queries]
+    rms_ref[...] = jnp.where(lane == 0, rms[0:1, :], rms[1:2, :])[:, 0:2]
+
+    for k in range(AHEAD):
+        @pl.when(is_inner)
+        def _():
+            outward_copy(total - 1 - k).wait_send()
+    for i in range(3):
+        tile_copy(i).wait_send()
+        gram_copy(i).wait_send()
+        for source in range(4):
+            proj_copy(i, source).wait_send()
+
+
+def piece_width(model_width, hidden_width):
+    for width in (512, 256, 128):
+        if model_width % (2 * width) == 0 and hidden_width % (2 * width) == 0:
+            return width
+    return 0
+
+
+def line_shards(width, activations, output_gradients, counts, left_factors, right_factors):
+    seq_dev, length, ff_local = activations.shape
+    model_local = output_gradients.shape[2]
+    row_count = seq_dev * length
+    columns = left_factors.shape[0]
+    n_left, n_right = model_local // (2 * width), ff_local // (2 * width)
+    pieces = n_left + n_right
+    dma = pltpu.SemaphoreType.DMA
+    anywhere = pl.BlockSpec(memory_space=pl.ANY)
+    vmem = pl.BlockSpec(memory_space=pltpu.VMEM)
+    scores, rms = pl.pallas_call(
+        functools.partial(line_kernel, n_left, n_right, width),
+        out_shape=(
+            jax.ShapeDtypeStruct((seq_dev, 4 * columns // RANK), jnp.float32),
+            jax.ShapeDtypeStruct((1, seq_dev), jnp.float32),
+        ),
+        in_specs=[pl.BlockSpec(memory_space=pltpu.SMEM)] + [anywhere] * 4,
+        out_specs=(vmem, vmem),
+        scratch_shapes=[
+            pltpu.VMEM((4, 2, pieces, columns, width), jnp.bfloat16),
+            pltpu.VMEM((2, pieces, row_count, width), jnp.bfloat16),
+            pltpu.VMEM((2, 4, columns, row_count), jnp.float32),
+            pltpu.VMEM((2, row_count, length), jnp.float32),
+            pltpu.VMEM((3, 4, columns, row_count), jnp.float32),
+            pltpu.VMEM((3, row_count, length), jnp.float32),
+            pltpu.VMEM((8, 128), jnp.float32),
+            pltpu.VMEM((3, 8, 128), jnp.float32),
+            dma((2, pieces)),
+            dma((2, pieces)),
+            dma((3 * pieces,)),
+            dma((2 * pieces,)),
+            dma((2, 3 * pieces)),
+            dma((3 * pieces,)),
+            dma((3 * pieces,)),
+            dma((3, 4)),
+            dma((3, 4)),
+            dma((3,)),
+            dma((3,)),
+            dma((3,)),
+            dma((3,)),
+        ],
+        compiler_params=pltpu.CompilerParams(
+            collective_id=0, has_side_effects=True, vmem_limit_bytes=32 * 2 ** 20
+        ),
+        cost_estimate=pl.CostEstimate(
+            flops=2 * row_count * (4 * columns + length) * (model_local + ff_local),
+            bytes_accessed=2 * (row_count + columns) * (model_local + ff_local),
+            transcendentals=0,
+        ),
+    )(
+        counts,
+        activations.reshape(row_count, ff_local),
+        output_gradients.reshape(row_count, model_local),
+        left_factors,
+        right_factors,
+    )
+    return scores, rms.reshape(seq_dev)
+
+
+def shards(sizes, activations, output_gradients, counts, left_factors, right_factors):
+    columns, model_local = left_factors.shape
+    width = piece_width(model_local, right_factors.shape[1])
+    fits = (
+        sizes == (2, 4, 4)
+        and width > 0
+        and columns % RANK == 0
+        and activations.shape[:2] == (2, 128)
+    )
+    run = functools.partial(line_shards, width) if fits else plain_shards
+    return run(activations, output_gradients, counts, left_factors, right_factors)
+
+
 def solution(mesh):
     placed = (
         P(("groups", "dp"), None, "mp"),
@@ -57,8 +399,9 @@
         P("dp", "mp"),
         P("dp", "mp"),
     )
+    sizes = tuple(mesh.shape[name] for name in ("groups", "dp", "mp"))
     return jax.shard_map(
-        shards,
+        functools.partial(shards, sizes),
         mesh=mesh,
         in_specs=placed,
         out_specs=(P(("groups", "dp"), None), P(("groups", "dp"))),

time: 168 us -> 62.7 us (0.37)
  waiting for transfers between devices: 133 us -> 0 us
  Pallas kernels: 0 us -> 54.6 us
  between operations: 13.8 us -> 0.65 us
  matrix products: 12.2 us -> 0 us
  blocking collectives: 7.02 us -> 0 us
  local copies, waits for them, and re-layouts: 1.35 us -> 7.11 us
    all_gather x2 -> x0, waiting for transfers between devices: 100 us -> none  [the longest x1 69.4 us: shards(): lax.all_gather(right_factors, 'dp', axis=0, tiled=True)]
    pallas_call x0 -> x1, Pallas kernels: none -> 54.6 us  [line_shards(): pl.pallas_call(functools.partial(line_kernel, n_left, n_right, width), ou...]
    psum x1 -> x0, waiting for transfers between devices: 31.5 us -> none  [shards(): lax.psum((grad_proj, gradient_covariance), 'mp')]
    dot_general x4 -> x0, matrix products: 12.2 us -> none  [the longest x2 6.69 us: contract_last(): lax.dot_general(left_side, right_side, (((1,), (1,)), ((), ())), preferre...]
    psum x1 -> x0, blocking collectives: 7.02 us -> none  [shards(): raw_score, norm_sq = lax.psum((score_part, norm_portion), 'mp')]
    unnamed x9 -> x12, local copies, waits for them, and re-layouts: 1.08 us -> 7.11 us
  transfers between devices with their start and end apart: 3 -> 0, of which waited for: 3 -> 0; matrix products, arithmetic and copies ran while one was open for 3% -> 0% of each run, Pallas kernels for 0% -> 0%
where the time goes in v1:
time: 62.7 us; the launch traced here: 62.4 us
  Pallas kernels  54.6 us (87%)
  local copies, waits for them, and re-layouts  7.11 us (11%)
  between operations  0.65 us (1%)
    pallas_call x1, Pallas kernels, line_shards(): pl.pallas_call(functools.partial(line_kernel, n_left, n_right, width), ou...  54.6 us
    unnamed x12, local copies, waits for them, and re-layouts  7.11 us

profile of v1, /device:TPU:0, one launch (start us, length us, event | category | flops | bytes accessed | tf_op | source)
XLA Modules:
  0.0 62.4 jit_solution(6366215665045958573)
XLA Ops:
  0.6 0.0 copy-start
  0.6 2.0 %copy-done = bf16[2,128,7168]{2,1,0:T(8,128)(2,1)S(1)} copy-done((bf16[2,128,7168]{2,1,0:T(8,128)(2,1)S(1)}, bf16[2,128,7168]{2,1,0:T(8,128)(2,1)}, u32[]{:S(2)}) %copy-start) | copy-done | bytes 3670040
  2.7 0.0 copy-start.1
  2.7 1.2 %copy-done.1 = bf16[2,128,2048]{2,1,0:T(8,128)(2,1)S(1)} copy-done((bf16[2,128,2048]{2,1,0:T(8,128)(2,1)S(1)}, bf16[2,128,2048]{2,1,0:T(8,128)(2,1)}, u32[]{:S(2)}) %copy-start.1) | copy-done | bytes 1048600
  3.9 0.0 copy-start.2
  3.9 1.2 %copy-done.2 = bf16[64,7168]{1,0:T(8,128)(2,1)S(1)} copy-done((bf16[64,7168]{1,0:T(8,128)(2,1)S(1)}, bf16[64,7168]{1,0:T(8,128)(2,1)}, u32[]{:S(2)}) %copy-start.2) | copy-done | bytes 917528
  5.1 0.0 copy-start.3
  5.1 0.9 %copy-done.3 = bf16[64,2048]{1,0:T(8,128)(2,1)S(1)} copy-done((bf16[64,2048]{1,0:T(8,128)(2,1)S(1)}, bf16[64,2048]{1,0:T(8,128)(2,1)}, u32[]{:S(2)}) %copy-start.3) | copy-done | bytes 262168
  6.0 0.0 copy-start.4
  6.0 0.7 %copy-done.4 = s32[2]{0:T(128)S(1)} copy-done((s32[2]{0:T(128)S(1)}, s32[2]{0:T(128)}, u32[]{:S(2)}) %copy-start.4) | copy-done | bytes 32
  6.7 54.6 %shard_map.68 = (f32[2,8]{1,0:T(2,128)S(1)}, f32[1,2]{1,0:T(1,128)S(1)}) custom-call(s32[2]{0:T(128)S(1)} %copy-done.4, bf16[256,7168]{1,0:T(8,128)(2,1)S(1)} %bitcast.3, bf16[256,2048]{1,0:T(8,128)(2,1)S(1)} %bitcast.4, bf16[64,2048]{1,0:T(8,128)(2,1)S(1)} %copy-done.3, bf16[64,7168]{1,0:T(8,128)(2,1)S(1)} %copy-done.2), custom_call_target="tpu_custom_call" | custom-call | flops 1811939328 | bytes 5898240 | tf_op jit(solution)/shard_map/pallas_call | solution.py:332
  61.3 0.6 copy.9
  61.9 0.5 copy.10
Async XLA Ops:
  0.6 2.0 %copy-start = (bf16[2,128,7168]{2,1,0:T(8,128)(2,1)S(1)}, bf16[2,128,7168]{2,1,0:T(8,128)(2,1)}, u32[]{:S(2)}) copy-start(bf16[2,128,7168]{2,1,0:T(8,128)(2,1)} %param.5) | copy-start | bytes 11010052
  2.7 1.2 %copy-start.1 = (bf16[2,128,2048]{2,1,0:T(8,128)(2,1)S(1)}, bf16[2,128,2048]{2,1,0:T(8,128)(2,1)}, u32[]{:S(2)}) copy-start(bf16[2,128,2048]{2,1,0:T(8,128)(2,1)} %param.6) | copy-start | bytes 3145732
  3.9 1.2 %copy-start.2 = (bf16[64,7168]{1,0:T(8,128)(2,1)S(1)}, bf16[64,7168]{1,0:T(8,128)(2,1)}, u32[]{:S(2)}) copy-start(bf16[64,7168]{1,0:T(8,128)(2,1)} %right_ref.1) | copy-start | bytes 2752516
  5.1 0.9 %copy-start.3 = (bf16[64,2048]{1,0:T(8,128)(2,1)S(1)}, bf16[64,2048]{1,0:T(8,128)(2,1)}, u32[]{:S(2)}) copy-start(bf16[64,2048]{1,0:T(8,128)(2,1)} %left_ref.1) | copy-start | bytes 786436
  6.0 0.7 %copy-start.4 = (s32[2]{0:T(128)S(1)}, s32[2]{0:T(128)}, u32[]{:S(2)}) copy-start(s32[2]{0:T(128)} %counts_ref.1) | copy-start | bytes 28

commit v2 on v1

--- a/solution.py
+++ b/solution.py
@@ -10,8 +10,8 @@
 D = 8192
 FF = 28672
 RANK = 32
-AHEAD = 3
-SWAP = 2
+AHEAD = 5
+SWAP = 3
 
 epsilon = 1e-06
 MESH = pl.DeviceIdType.MESH
@@ -58,8 +58,8 @@
 def line_kernel(
     n_left, n_right, width,
     counts_ref, act_ref, grad_ref, left_ref, right_ref,
-    scores_ref, rms_ref,
-    factors, rows, proj, gram, proj_in, gram_in, tile, tile_in,
+    out_ref,
+    factors, rows, proj, gram, proj_in, gram_in, full, found, tile, tile_in,
     own_sem, row_sem, out_send, in_send, line_recv, swap_send, swap_recv,
     proj_send, proj_recv, gram_send, gram_recv, tile_send, tile_recv,
 ):
@@ -89,27 +89,25 @@
             source.at[:, at:at + width], rows.at[half, piece], row_sem.at[half, piece]
         )
 
+    barrier = pltpu.get_barrier_semaphore()
+    for i in range(3):
+        pl.semaphore_signal(barrier, inc=1, device_id=(g, z, peers[i]), device_id_type=MESH)
+    pl.semaphore_signal(barrier, inc=1, device_id=(other, z, m), device_id_type=MESH)
+    pl.semaphore_signal(barrier, inc=1, device_id=(g, inward, m), device_id_type=MESH)
+
+    @pl.when(is_inner)
+    def _():
+        pl.semaphore_signal(barrier, inc=1, device_id=(g, outward, m), device_id_type=MESH)
+
     everything = [(half, piece) for piece in range(pieces) for half in range(2)]
     for half, piece in everything:
         factor_copy(half, piece).start()
     for half, piece in everything:
         row_copy(half, piece).start()
 
-    barrier = pltpu.get_barrier_semaphore()
-    for i in range(3):
-        pl.semaphore_signal(barrier, inc=1, device_id=(g, z, peers[i]), device_id_type=MESH)
-    pl.semaphore_signal(barrier, inc=1, device_id=(other, z, m), device_id_type=MESH)
-    pl.semaphore_signal(barrier, inc=1, device_id=(g, inward, m), device_id_type=MESH)
-
-    @pl.when(is_inner)
-    def _():
-        pl.semaphore_signal(barrier, inc=1, device_id=(g, outward, m), device_id_type=MESH)
-
     proj[...] = jnp.zeros_like(proj)
     gram[...] = jnp.zeros_like(gram)
     pl.semaphore_wait(barrier, 5 + inner)
-    for half, piece in everything:
-        factor_copy(half, piece).wait()
 
     def outward_copy(k):
         block = factors.at[(z + (k // pieces) * step_in) % 4, g, k % pieces]
@@ -192,6 +190,13 @@
     total = 3 * pieces
 
     def step(k, carry):
+        @pl.when(k < pieces)
+        def _():
+            for half in range(2):
+                pltpu.make_async_copy(
+                    left_ref.at[:, 0:width], factors.at[z, half, k], own_sem.at[half, k]
+                ).wait()
+
         @pl.when(k < total)
         def _():
             @pl.when(is_inner)
@@ -257,49 +262,68 @@
                     proj_copy(i, main_source(j)).start()
         return carry
 
-    lax.fori_loop(0, total + AHEAD + SWAP, step, 0)
-
+    columns = proj.shape[2]
+    share = columns // RANK
     token = lax.broadcasted_iota(jnp.int32, (1, length), 1)
     masks = [(token < counts_ref[seq]).astype(jnp.float32) for seq in range(2)]
-    row_token = lax.broadcasted_iota(jnp.int32, (length, 1), 0)
-    row_masks = [(row_token < counts_ref[seq]).astype(jnp.float32) for seq in range(2)]
-    for i in range(3):
-        gram_copy(i).wait_recv()
-    norms = []
+    mask_row = jnp.concatenate(masks, axis=1)
+    lane = lax.broadcasted_iota(jnp.int32, (8, 128), 1)
+    sublane = lax.broadcasted_iota(jnp.int32, (8, 128), 0)
+
+    def norm_terms():
+        row_token = lax.broadcasted_iota(jnp.int32, (length, 1), 0)
+        for i in range(3):
+            gram_copy(i).wait_recv()
+        kept = jnp.zeros((8, 128), jnp.float32)
+        for seq in range(2):
+            span = slice(seq * length, (seq + 1) * length)
+            whole = gram[0, span, :] + gram_in[0, span, :] + gram_in[1, span, :] + gram_in[2, span, :]
+            valid = (row_token < counts_ref[seq]).astype(jnp.float32)
+            terms = whole * gram[1, span, :] * masks[seq] * valid
+            down = jnp.sum(terms, axis=0, keepdims=True)
+            kept += jnp.where(lane == 2 + seq, jnp.sum(down, axis=1, keepdims=True), 0.0)
+        tile[...] = kept
+
+    def take_projections(source):
+        for i in range(3):
+            proj_copy(i, source).wait_recv()
+        whole = proj_in[0, source] + proj_in[1, source] + proj_in[2, source]
+        full[source] = (proj[0, source] + whole) * mask_row
+
+    def score_terms(source):
+        terms = full[source] * proj[1, source]
+        row = lax.broadcasted_iota(jnp.int32, (8, 2 * length), 0)
+        for q in range(share):
+            down = jnp.sum(terms[q * RANK:(q + 1) * RANK, :], axis=0, keepdims=True)
+            found[...] += jnp.where(row == source * share + q, down, 0.0)
+
+    found[...] = jnp.zeros_like(found)
+    lax.fori_loop(0, total + AHEAD + SWAP - 2, step, 0)
+    norm_terms()
+    take_projections(z)
+    score_terms(z)
+    for phase in range(3):
+        take_projections(main_source(phase * pieces))
+    for phase in range(2):
+        score_terms(main_source(phase * pieces))
+    lax.fori_loop(total + AHEAD + SWAP - 2, total + AHEAD + SWAP, step, 0)
+    score_terms(main_source(2 * pieces))
+    mine = tile[...]
     for seq in range(2):
         span = slice(seq * length, (seq + 1) * length)
-        whole = gram[0, span, :] + gram_in[0, span, :] + gram_in[1, span, :] + gram_in[2, span, :]
-        terms = whole * gram[1, span, :] * masks[seq]
-        down = jnp.sum(terms * row_masks[seq], axis=0, keepdims=True)
-        norms.append(jnp.sum(down, axis=1, keepdims=True))
-    for i in range(3):
-        for source in range(4):
-            proj_copy(i, source).wait_recv()
-    columns = proj.shape[2]
-    queries = 4 * columns // RANK
-    mask_row = jnp.concatenate(masks, axis=1)
-    lane = lax.broadcasted_iota(jnp.int32, (1, 128), 1)
-    found = [jnp.zeros((1, 128), jnp.float32) for _ in range(2)]
-    for source in range(4):
-        whole = proj[0, source] + proj_in[0, source] + proj_in[1, source] + proj_in[2, source]
-        terms = whole * proj[1, source] * mask_row
-        for q in range(columns // RANK):
-            down = jnp.sum(terms[q * RANK:(q + 1) * RANK, :], axis=0, keepdims=True)
-            for seq in range(2):
-                value = jnp.sum(down[:, seq * length:(seq + 1) * length], axis=1, keepdims=True)
-                found[seq] += jnp.where(lane == source * (columns // RANK) + q, value, 0.0)
-    tile[...] = jnp.concatenate(
-        found + [jnp.broadcast_to(norms[seq], (1, 128)) for seq in range(2)]
-        + [jnp.zeros((4, 128), jnp.float32)], axis=0
-    )
+        value = jnp.sum(found[:, span], axis=1, keepdims=True)
+        mine += jnp.where(lane == seq, value, 0.0)
+    tile[...] = mine
     for i in range(3):
         tile_copy(i).start()
     for i in range(3):
         tile_copy(i).wait_recv()
     whole = tile[...] + tile_in[0] + tile_in[1] + tile_in[2]
-    rms = jnp.sqrt(whole[2:4, :] / (D * FF) + epsilon)
-    scores_ref[...] = (whole[0:2, :] / rms)[:, 0:queries]
-    rms_ref[...] = jnp.where(lane == 0, rms[0:1, :], rms[1:2, :])[:, 0:2]
+    rms = jnp.sqrt(whole[0:1, 2:4] / (D * FF) + epsilon)
+    for seq in range(2):
+        score = jnp.sum(jnp.where(lane == sublane, whole[:, seq:seq + 1], 0.0), axis=0, keepdims=True)
+        out_ref[seq:seq + 1, :] = score / rms[:, seq:seq + 1]
+    out_ref[2:3, 0:2] = rms
 
     for k in range(AHEAD):
         @pl.when(is_inner)
@@ -310,6 +334,11 @@
         gram_copy(i).wait_send()
         for source in range(4):
             proj_copy(i, source).wait_send()
+
+
+def take_out(result_ref, scores_ref, rms_ref):
+    scores_ref[...] = result_ref[0:scores_ref.shape[0], 0:scores_ref.shape[1]]
+    rms_ref[...] = result_ref[2:3, 0:rms_ref.shape[1]]
 
 
 def piece_width(model_width, hidden_width):
@@ -329,14 +358,11 @@
     dma = pltpu.SemaphoreType.DMA
     anywhere = pl.BlockSpec(memory_space=pl.ANY)
     vmem = pl.BlockSpec(memory_space=pltpu.VMEM)
-    scores, rms = pl.pallas_call(
+    result = pl.pallas_call(
         functools.partial(line_kernel, n_left, n_right, width),
-        out_shape=(
-            jax.ShapeDtypeStruct((seq_dev, 4 * columns // RANK), jnp.float32),
-            jax.ShapeDtypeStruct((1, seq_dev), jnp.float32),
-        ),
+        out_shape=jax.ShapeDtypeStruct((8, 128), jnp.float32),
         in_specs=[pl.BlockSpec(memory_space=pltpu.SMEM)] + [anywhere] * 4,
-        out_specs=(vmem, vmem),
+        out_specs=vmem,
         scratch_shapes=[
             pltpu.VMEM((4, 2, pieces, columns, width), jnp.bfloat16),
             pltpu.VMEM((2, pieces, row_count, width), jnp.bfloat16),
@@ -344,6 +370,8 @@
             pltpu.VMEM((2, row_count, length), jnp.float32),
             pltpu.VMEM((3, 4, columns, row_count), jnp.float32),
             pltpu.VMEM((3, row_count, length), jnp.float32),
+            pltpu.VMEM((4, columns, row_count), jnp.float32),
+            pltpu.VMEM((8, row_count), jnp.float32),
             pltpu.VMEM((8, 128), jnp.float32),
             pltpu.VMEM((3, 8, 128), jnp.float32),
             dma((2, pieces)),
@@ -361,7 +389,7 @@
             dma((3,)),
         ],
         compiler_params=pltpu.CompilerParams(
-            collective_id=0, has_side_effects=True, vmem_limit_bytes=32 * 2 ** 20
+            collective_id=0, has_side_effects=True, vmem_limit_bytes=60 * 2 ** 20
         ),
         cost_estimate=pl.CostEstimate(
             flops=2 * row_count * (4 * columns + length) * (model_local + ff_local),
@@ -375,6 +403,13 @@
         left_factors,
         right_factors,
     )
+    scores, rms = pl.pallas_call(
+        take_out,
+        out_shape=(
+            jax.ShapeDtypeStruct((seq_dev, 4 * columns // RANK), jnp.float32),
+            jax.ShapeDtypeStruct((1, seq_dev), jnp.float32),
+        ),
+    )(result)
     return scores, rms.reshape(seq_dev)
 
 
@@ -384,7 +419,8 @@
     fits = (
         sizes == (2, 4, 4)
         and width > 0
-        and columns % RANK == 0
+        and columns == 2 * RANK
+        and right_factors.shape[1] // (2 * width) > AHEAD
         and activations.shape[:2] == (2, 128)
     )
     run = functools.partial(line_shards, width) if fits else plain_shards

time: 62.7 us -> 56.1 us (0.89)
  local copies, waits for them, and re-layouts: 7.11 us -> 0 us
    unnamed x12 -> x0, local copies, waits for them, and re-layouts: 7.11 us -> none
    pallas_call x0 -> x1, Pallas kernels: none -> 1.24 us  [line_shards(): pl.pallas_call(take_out, out_shape=(jax.ShapeDtypeStruct((seq_dev, 4 * co...]
    pallas_call x1, Pallas kernels: 54.6 us -> 54 us  [line_shards(): pl.pallas_call(functools.partial(line_kernel, n_left, n_right, width), ou...]
where the time goes in v2:
time: 56.1 us; the launch traced here: 55.9 us
  Pallas kernels  55.2 us (98%)
  between operations  0.64 us (1%)
    pallas_call x1, Pallas kernels, line_shards(): pl.pallas_call(functools.partial(line_kernel, n_left, n_right, width), ou...  54 us
    pallas_call x1, Pallas kernels, line_shards(): pl.pallas_call(take_out, out_shape=(jax.ShapeDtypeStruct((seq_dev, 4 * co...  1.24 us

profile of v2, /device:TPU:0, one launch (start us, length us, event | category | flops | bytes accessed | tf_op | source)
XLA Modules:
  0.0 55.9 jit_solution(2510360136860842659)
XLA Ops:
  0.6 54.0 %shard_map.68.result_ref = f32[8,128]{1,0:T(8,128)} custom-call(s32[2]{0:T(128)} %counts_ref.1, bf16[256,7168]{1,0:T(8,128)(2,1)} %bitcast.3, bf16[256,2048]{1,0:T(8,128)(2,1)} %bitcast.4, bf16[64,2048]{1,0:T(8,128)(2,1)} %left_ref.1, bf16[64,7168]{1,0:T(8,128)(2,1)} %right_ref.1), custom_call_target="tpu_custom_call" | custom-call | flops 1811939328 | bytes 5898240 | tf_op jit(solution)/shard_map/pallas_call | solution.py:361
  54.6 1.2 %shard_map.69 = (f32[2,8]{1,0:T(2,128)}, f32[1,2]{1,0:T(1,128)}) custom-call(f32[8,128]{1,0:T(8,128)} %shard_map.68.result_ref), custom_call_target="tpu_custom_call" | custom-call | tf_op jit(solution)/shard_map/pallas_call | solution.py:406

commit v3 on v2

--- a/solution.py
+++ b/solution.py
@@ -102,8 +102,6 @@
     everything = [(half, piece) for piece in range(pieces) for half in range(2)]
     for half, piece in everything:
         factor_copy(half, piece).start()
-    for half, piece in everything:
-        row_copy(half, piece).start()
 
     proj[...] = jnp.zeros_like(proj)
     gram[...] = jnp.zeros_like(gram)
@@ -189,7 +187,7 @@
     length = rows.shape[2] // 2
     total = 3 * pieces
 
-    def step(k, carry):
+    def send_step(k, carry):
         @pl.when(k < pieces)
         def _():
             for half in range(2):
@@ -214,9 +212,14 @@
             def _():
                 inward_copy(k).start()
 
-        @pl.when((k >= AHEAD) & (k < total + AHEAD))
-        def _():
-            j = k - AHEAD
+        return carry
+
+    def step(k, carry):
+        send_step(k + AHEAD, 0)
+
+        @pl.when(k < total)
+        def _():
+            j = k
 
             @pl.when(j < 2 * pieces + (1 - inner) * pieces)
             def _():
@@ -246,9 +249,9 @@
                 proj_copy(i, z).start()
                 gram_copy(i).start()
 
-        @pl.when(k >= AHEAD + SWAP)
-        def _():
-            j = k - AHEAD - SWAP
+        @pl.when(k >= SWAP)
+        def _():
+            j = k - SWAP
 
             @pl.when(j < 2 * pieces + (1 - inner) * pieces)
             def _():
@@ -298,7 +301,10 @@
             found[...] += jnp.where(row == source * share + q, down, 0.0)
 
     found[...] = jnp.zeros_like(found)
-    lax.fori_loop(0, total + AHEAD + SWAP - 2, step, 0)
+    lax.fori_loop(0, AHEAD, send_step, 0)
+    for half, piece in everything:
+        row_copy(half, piece).start()
+    lax.fori_loop(0, total + SWAP - 2, step, 0)
     norm_terms()
     take_projections(z)
     score_terms(z)
@@ -306,7 +312,7 @@
         take_projections(main_source(phase * pieces))
     for phase in range(2):
         score_terms(main_source(phase * pieces))
-    lax.fori_loop(total + AHEAD + SWAP - 2, total + AHEAD + SWAP, step, 0)
+    lax.fori_loop(total + SWAP - 2, total + SWAP, step, 0)
     score_terms(main_source(2 * pieces))
     mine = tile[...]
     for seq in range(2):

time: 56.1 us -> 56.1 us (level)
  no operation moved by 1% of the time
where the time goes in v3:
time: 56.1 us; the launch traced here: 55.9 us
  Pallas kernels  55.2 us (98%)
  between operations  0.64 us (1%)
    pallas_call x1, Pallas kernels, line_shards(): pl.pallas_call(functools.partial(line_kernel, n_left, n_right, width), ou...  54 us
    pallas_call x1, Pallas kernels, line_shards(): pl.pallas_call(take_out, out_shape=(jax.ShapeDtypeStruct((seq_dev, 4 * co...  1.24 us

profile of v3, /device:TPU:0, one launch (start us, length us, event | category | flops | bytes accessed | tf_op | source)
XLA Modules:
  0.0 55.9 jit_solution(3079402713158834657)
XLA Ops:
  0.6 54.0 %shard_map.68.result_ref = f32[8,128]{1,0:T(8,128)} custom-call(s32[2]{0:T(128)} %counts_ref.1, bf16[256,7168]{1,0:T(8,128)(2,1)} %bitcast.3, bf16[256,2048]{1,0:T(8,128)(2,1)} %bitcast.4, bf16[64,2048]{1,0:T(8,128)(2,1)} %left_ref.1, bf16[64,7168]{1,0:T(8,128)(2,1)} %right_ref.1), custom_call_target="tpu_custom_call" | custom-call | flops 1811939328 | bytes 5898240 | tf_op jit(solution)/shard_map/pallas_call | solution.py:367
  54.6 1.2 %shard_map.69 = (f32[2,8]{1,0:T(2,128)}, f32[1,2]{1,0:T(1,128)}) custom-call(f32[8,128]{1,0:T(8,128)} %shard_map.68.result_ref), custom_call_target="tpu_custom_call" | custom-call | tf_op jit(solution)/shard_map/pallas_call | solution.py:412
